TPU v7x, 32 devices: a whole 2x2x4 slice. The times are simulated.
32 devices in a mesh: dp: 2 (over x), blk: 4 (over z), tensor: 4 (over y, core).
Axes of the slice: x: 2, y: 2, z: 4, core: 2. Of those that a mesh axis runs over, the one named last changes fastest.
Arguments:
- block_input: bfloat16 [4, 2048, 2048], P('dp', 'blk', 'tensor'), may hold values from -6 to 6
- segment_ids: int32 [4, 2048], P('dp'), may hold values from 0 to 7, as said below
- layer_norm_gain: float32 [2048], replicated, may hold values from 0.5 to 1.5
- layer_norm_bias: float32 [2048], replicated, may hold values from -4 to 4
- qkv_weight: bfloat16 [2048, 3, 2048], P(None, None, 'tensor'), may hold values from -0.125 to 0.125
- qkv_bias: float32 [3, 2048], P(None, 'tensor'), may hold values from -0.4375 to 0.4375
- out_weight: bfloat16 [2048, 2048], P('tensor'), may hold values from -2 to 2
- out_bias: float32 [2048], P('tensor'), may hold values from -4 to 4
- up_weight: bfloat16 [2048, 8192], P(None, 'tensor'), may hold values from -0.125 to 0.125
- up_bias: float32 [8192], P('tensor'), may hold values from -4 to 4
- down_weight: bfloat16 [8192, 2048], P('tensor'), may hold values from -0.0625 to 0.0625
- down_bias: float32 [2048], P('tensor'), may hold values from -4 to 4
- grad_output: bfloat16 [4, 2048, 2048], P('dp', 'blk', 'tensor'), may hold values from -6 to 6
Outputs:
- block_output: bfloat16 [4, 2048, 2048], P('dp', 'blk', 'tensor')
- input_grad: bfloat16 [4, 2048, 2048], P('dp', 'blk', 'tensor')
- norm_gain_grad: float32 [2048], P('tensor')
- norm_bias_grad: float32 [2048], P('tensor')
- qkv_weight_grad: float32 [2048, 3, 2048], P(None, None, 'tensor')
- qkv_bias_grad: float32 [3, 2048], P(None, 'tensor')
- out_weight_grad: float32 [2048, 2048], P('tensor')
- out_bias_grad: float32 [2048], P('tensor')
- up_weight_grad: float32 [2048, 8192], P(None, 'tensor')
- up_bias_grad: float32 [8192], P('tensor')
- down_weight_grad: float32 [8192, 2048], P('tensor')
- down_bias_grad: float32 [2048], P('tensor')
Inputs may be any that keep to these rules, and one draw needn't show every extreme that they name: `segment_ids`: segment ids never fall along a row; each row uses every id from 0 to 7, and in each row one document holds every position from 256 to 1792.
All inputs are finite; a program needn't handle non-finite values.
Results may differ from a plain program's by a relative error of at most 0.02.
Values may be sent and summed in bfloat16 or wider, within the bound.
A program may use at most 320 MiB of HBM per device.

v0:
```python
import functools
import math

import jax
import jax.numpy as jnp
import numpy as np
from jax import lax
from jax.experimental import pallas as pl
from jax.experimental.pallas import tpu as pltpu
from jax.sharding import PartitionSpec as P

HD = 64
ROT = 32
EPSILON = 1e-05
ROPE_LOG_BASE = math.log(10000.0)
NEGATIVE = -1e30
F32 = jnp.float32
BF = jnp.bfloat16
MESH = pl.DeviceIdType.MESH
dot32 = functools.partial(jnp.dot, preferred_element_type=F32)


def swap(value, axis, size, mask):
    return lax.ppermute(value, axis, [(i, i ^ mask) for i in range(size)])


def flip(index, mask):
    if mask == 0:
        return index
    if mask == 1:
        return index + 1 - 2 * (index % 2)
    if mask == 2:
        return (index + 2) % 4
    return 3 - index


def core_share(cross_ref, stage, cross_sems, stage_sems, tokens, t, value, out, between=None):
    _, many, width = out.shape
    blocks = many // tokens
    core = t % 2

    def place(k):
        return pl.ds(pl.multiple_of((k % blocks) * tokens, tokens), tokens)

    def tile(slot, k):
        return stage.at[k % 2, :, pl.ds(slot * width, width)]

    def at(ref, k):
        return ref.at[k // blocks, place(k)]

    def columns(k, of_core):
        return pl.ds(pl.multiple_of((2 * (k // blocks) + of_core) * width, width), width)

    def cross(k, src, dst):
        return pltpu.make_async_remote_copy(
            src, dst, cross_sems.at[0, k], cross_sems.at[1, k], device_id={"tensor": flip(t, 1)}, device_id_type=MESH
        )

    def give(k):
        return cross(k, tile(0, k), at(cross_ref, k))

    def got(k):
        return cross(k, at(cross_ref, k), at(cross_ref, k))

    def fetch(k):
        return pltpu.make_async_copy(at(cross_ref, k), tile(1, k), stage_sems.at[k % 2])

    def keep(k):
        return pltpu.make_async_copy(tile(2, k), at(out, k), stage_sems.at[2 + k % 2])

    @pl.loop(0, 2 * blocks)
    def _(k):
        @pl.when(k >= 2)
        def _():
            give(k - 2).wait_send()

        stage[k % 2, :, :width] = value(place(k), columns(k, 1 - core)).astype(BF)
        give(k).start()

    for k in (2 * blocks - 2, 2 * blocks - 1):
        give(k).wait_send()
    if between:
        between()
    got(0).wait_recv()
    fetch(0).start()

    @pl.loop(0, 2 * blocks)
    def _(k):
        @pl.when(k >= 2)
        def _():
            keep(k - 2).wait()

        @pl.when(k + 1 < 2 * blocks)
        def _():
            got(k + 1).wait_recv()
            fetch(k + 1).start()

        mine = value(place(k), columns(k, core))
        fetch(k).wait()
        stage[k % 2, :, 2 * width : 3 * width] = (mine + stage[k % 2, :, width : 2 * width].astype(F32)).astype(BF)
        keep(k).start()

    for k in (2 * blocks - 2, 2 * blocks - 1):
        keep(k).wait()


def front_kernel(
    gather, split, rows, tokens, segments_ref, frequency_ref, x_own, g_own, gain_ref, shift_ref, wq_ref, bq_ref, wo_ref, wu_ref, bu_ref, wd_ref,
    normed_o, g_o, land_o, stats_o, down_o, d_hidden_o, branch_o, ubias_o, cos_o, sin_o, start_o, branch_y_o, cross_o,
    xin, gin, vq, vo, vu, vd, pay, act, slope, stage, gather_sems, land_sems, load_sems, keep_sems, stage_sems, cross_sems, over_y_sems, segments, segment_sems,
):
    x, z, t = lax.axis_index("dp"), lax.axis_index("blk"), lax.axis_index("tensor")
    many, features = xin.shape
    half = rows * tokens
    width = features // 4
    att = vq.shape[2]
    ff = vu.shape[1]
    nz = pay.shape[0]
    wide = min(512, ff)

    def remote(src, dst, sems, device):
        return pltpu.make_async_remote_copy(
            src, dst, sems[0], sems[1], device_id=device, device_id_type=MESH
        )

    peers = {"x": {"dp": 1 - x}, "y": {"tensor": flip(t, 2)}, "c": {"tensor": flip(t, 1)}}
    barrier = pltpu.get_barrier_semaphore()
    greet = [{"blk": flip(z, m)} for m in range(1, nz)] + (list(peers.values()) if gather else [peers["x"]])
    for device in greet:
        pl.semaphore_signal(barrier, inc=1, device_id=device, device_id_type=MESH)

    loads = [
        pltpu.make_async_copy(
            wq_ref.at[:, :, pl.ds(pl.multiple_of(x * att, 128), att)] if split else wq_ref, vq, load_sems.at[0]
        ),
        pltpu.make_async_copy(
            wu_ref.at[:, pl.ds(pl.multiple_of(x * ff, 128), ff)] if split else wu_ref, vu, load_sems.at[1]
        ),
        pltpu.make_async_copy(wd_ref.at[pl.ds(x * ff, ff)] if split else wd_ref, vd, load_sems.at[2]),
        pltpu.make_async_copy(wo_ref.at[pl.ds(x * att, att)] if split else wo_ref, vo, load_sems.at[3]),
    ]
    if not gather:
        both = [
            pltpu.make_async_copy(x_own, xin, load_sems.at[4]),
            pltpu.make_async_copy(g_own, gin, load_sems.at[5]),
        ]
    else:
        both = [
            pltpu.make_async_copy(
                own,
                buf.at[pl.ds(x * half, half), pl.ds(pl.multiple_of(t * width, 128), width)],
                load_sems.at[4 + i],
            )
            for i, (own, buf) in enumerate([(x_own, xin), (g_own, gin)])
        ]
    both[0].start()
    both[1].start()
    pl.semaphore_wait(barrier, len(greet))

    class Gather:
        def __init__(self, which, own, buf, first, size):
            self.which, self.own, self.buf, self.names = which, own, buf, []
            self.base, self.size = first, size

        def at(self, dx, dt, r):
            return self.buf.at[
                pl.ds(pl.multiple_of((1 - x if dx else x) * half + self.base + r * self.size, self.size), self.size),
                pl.ds(pl.multiple_of(flip(t, dt) * width, 128), width),
            ]

        plan = {
            "x": (0, 0, "x", 1, 0), "y": (0, 0, "y", 0, 2), "c": (0, 0, "c", 0, 1),
            "ex": (1, 0, "c", 1, 1), "ey": (0, 2, "c", 0, 3), "ed": (1, 2, "c", 1, 3),
        }

        def sems(self, kind, r):
            k = 2 * ("x", "y", "c", "d", "ex", "ey", "ed").index(kind) + r
            return gather_sems.at[self.which, 0, k], gather_sems.at[self.which, 1, k]

        def copy(self, kind, r):
            if kind == "d":
                dx, dt, to = (1, 0, "y") if r == 0 else (0, 2, "x")
            else:
                dx, dt, to = self.plan[kind][:3]
            src = dst = self.at(dx, dt, r)
            if kind in "xyc":
                src = self.own.at[pl.ds(self.base + r * self.size, self.size)]
            return remote(src, dst, self.sems(kind, r), peers[to])

        def start(self, kind, r):
            self.names.append((kind, r))
            self.copy(kind, r).start()

        def wait(self, kind, r):
            if kind == "d":
                dx, dt, to = 1, 2, "y"
            else:
                to, dx, dt = self.plan[kind][2:]
            ref = self.at(dx, dt, r)
            remote(ref, ref, self.sems(kind, r), peers[to]).wait_recv()

        def begin(self):
            for kind, r in (("x", 0), ("y", 1), ("x", 1), ("y", 0), ("c", 0), ("c", 1)):
                self.start(kind, r)

        def second(self):
            self.wait("x", 0)
            self.start("d", 0)
            self.start("ex", 0)
            self.wait("y", 1)
            self.start("d", 1)
            self.start("ey", 1)

        def third(self):
            self.wait("x", 1)
            self.start("ex", 1)
            self.wait("y", 0)
            self.start("ey", 0)

        def fourth(self):
            self.wait("d", 0)
            self.start("ed", 0)
            self.wait("d", 1)
            self.start("ed", 1)

        def last(self):
            for kind in ("c", "ex", "ey", "ed"):
                for r in range(2):
                    self.wait(kind, r)

        def drain(self):
            for kind, r in self.names:
                self.copy(kind, r).wait_send()

    ins = [Gather(r, x_own, xin, r * tokens, tokens // 2) for r in range(rows)]
    cots = Gather(rows, g_own, gin, 0, half // 2)
    own_segments = pltpu.make_async_copy(segments_ref, segments.at[x], segment_sems.at[0])
    own_segments.start()
    segments_x = remote(segments_ref, segments.at[x], (segment_sems.at[1], segment_sems.at[2]), peers["x"])
    segments_x.start()
    if gather:
        ins[0].begin()
    for load in loads:
        load.start()

    own_segments.wait()
    segments_x.wait()
    ids = segments[z // rows]
    length = ids.shape[1]
    ids = jnp.sum(jnp.where(lax.broadcasted_iota(jnp.int32, ids.shape, 0) == z % rows, ids, 0), axis=0, keepdims=True)
    ids = jnp.broadcast_to(ids, (8, length))
    at = lax.broadcasted_iota(jnp.int32, (8, length), 1)
    first_of = jnp.where(ids != pltpu.roll(ids, 1, 1), at, 0)
    reach = 1
    while reach < length:
        first_of = jnp.maximum(first_of, jnp.where(at >= reach, pltpu.roll(first_of, reach, 1), 0))
        reach *= 2
    start_o[...] = first_of
    angles = frequency_ref[...] * (at - first_of)[0:1].astype(F32)
    cos_o[...] = jnp.cos(angles)
    sin_o[...] = jnp.sin(angles)

    def place(position):
        return pl.ds(pl.multiple_of(position * tokens, tokens), tokens)

    def normalize(row):
        @pl.loop(0, tokens // 128)
        def _(i):
            at = pl.ds(pl.multiple_of(row * tokens + i * 128, 128), 128)
            v = xin[at, :].astype(F32)
            mean = jnp.sum(v, axis=-1, keepdims=True) * (1.0 / features)
            v = v - mean
            inverse = lax.rsqrt(jnp.sum(v * v, axis=-1, keepdims=True) * (1.0 / features) + EPSILON)
            xin[at, :] = (v * inverse * gain_ref[...] + shift_ref[...]).astype(BF)
            lane = lax.broadcasted_iota(jnp.int32, (128, 128), 1)
            stats_o[at, :] = jnp.where(lane < 64, mean, inverse)

    def parts(kind):
        return pl.ds(0, 3) if kind == 0 else pl.ds(3, 1)

    def sems(kind, m):
        return land_sems.at[0, kind, m], land_sems.at[1, kind, m]

    def own_row(kind):
        return pltpu.make_async_copy(
            pay.at[z, parts(kind)], land_o.at[parts(kind), place(z)], keep_sems.at[2 + kind]
        )

    def other_row(kind, row, m):
        return remote(pay.at[row, parts(kind)], land_o.at[parts(kind), place(z)], sems(kind, m), {"blk": row})

    def send(kind, row):
        @pl.when(z == row)
        def _():
            own_row(kind).start()

        @pl.when(z != row)
        def _():
            other_row(kind, row, flip(z, row)).start()

    def landed(kind, m):
        ref = land_o.at[parts(kind), place(flip(z, m))]
        return remote(ref, ref, sems(kind, m), {"blk": flip(z, m)})

    def project(row):
        @pl.loop(0, 3)
        def _(part):
            bias = bq_ref[part, :, pl.ds(pl.multiple_of(x * att, 128), att)] if split else bq_ref[part]
            value = dot32(xin[place(row), :], vq[part]) + bias
            pay[row, part] = value.astype(BF)

        send(0, row)

    if gather:
        ins[0].second()
        ins[0].third()
        ins[1].begin()
        ins[0].fourth()
    both[0].wait()
    for r in range(rows):
        if gather:
            ins[r].last()
            ins[r].drain()
        for row in range(r, nz, rows):
            normalize(row)
        if gather and r == 0:
            ins[1].second()
        if r == 0:
            loads[0].wait()
        for row in range(r, nz, rows):
            project(row)
        if gather and r == 0:
            ins[1].third()
            cots.begin()
            ins[1].fourth()
    keep_normed = pltpu.make_async_copy(xin, normed_o, keep_sems.at[0])
    keep_normed.start()
    if gather:
        cots.second()

    loads[1].wait()

    @pl.loop(0, many // tokens)
    def _(i):
        at = place(i)

        @pl.loop(0, ff // wide)
        def _(j):
            columns = pl.ds(pl.multiple_of(j * wide, wide), wide)
            first = x * ff if split else 0
            h = dot32(xin[at, :], vu[:, columns]) + bu_ref[:, pl.ds(pl.multiple_of(first + j * wide, wide), wide)]
            c = math.sqrt(2.0 / math.pi)
            square = h * h
            tanh = jnp.tanh(c * h * (1.0 + 0.044715 * square))
            one = 0.5 * (1.0 + tanh)
            act[at, columns] = (h * one).astype(BF)
            d = one + 0.5 * h * (1.0 - tanh * tanh) * (c * (1.0 + 3 * 0.044715 * square))
            slope[at, columns] = d.astype(BF)

    if gather:
        cots.third()
    nt_dims = (((1,), (1,)), ((), ()))
    tn_dims = (((0,), (0,)), ((), ()))
    general = functools.partial(lax.dot_general, preferred_element_type=F32)

    def through(steps, rows_of, columns_of, make, out):
        def copy(i):
            return pltpu.make_async_copy(
                stage.at[i % 2, pl.ds(0, rows_of), pl.ds(0, columns_of)],
                out.at[pl.ds(pl.multiple_of(i * rows_of, rows_of), rows_of)],
                stage_sems.at[i % 2],
            )

        @pl.loop(0, steps)
        def _(i):
            @pl.when(i >= 2)
            def _():
                copy(i - 2).wait()

            make(i, stage.at[i % 2, pl.ds(0, rows_of), pl.ds(0, columns_of)])
            copy(i).start()

        for i in range(max(0, steps - 2), steps):
            copy(i).wait()

    loads[2].wait()
    if gather:
        core_share(
            cross_o, stage, cross_sems, stage_sems, tokens, t,
            lambda at, columns: dot32(act[at, :], vd[:, columns]), branch_o,
        )
        branch_over_y = remote(
            branch_o.at[1 - t // 2, pl.ds(0, half)], branch_y_o, (over_y_sems.at[0], over_y_sems.at[1]), peers["y"]
        )
        branch_over_y.start()
    else:

        def whole(i, target):
            @pl.loop(0, features // 512)
            def _(j):
                columns = pl.ds(pl.multiple_of(j * 512, 512), 512)
                target[:, columns] = dot32(act[place(i), :], vd[:, columns]).astype(BF)

        through(many // tokens, tokens, features, whole, branch_o)

    if gather:
        cots.fourth()
    both[1].wait()
    if gather:
        cots.last()
    keep_g = pltpu.make_async_copy(gin, g_o, keep_sems.at[1])
    keep_g.start()

    loads[3].wait()
    for row in range(nz):
        pay[row, 3] = general(gin[place(row), :], vo[...], nt_dims).astype(BF)
        send(1, row)

    ubias_o[...] = jnp.zeros_like(ubias_o)

    @pl.loop(0, many // tokens)
    def _(i):
        at = place(i)

        @pl.loop(0, ff // wide)
        def _(j):
            columns = pl.ds(pl.multiple_of(j * wide, wide), wide)
            d = general(gin[at, :], vd[columns, :], nt_dims) * slope[at, columns].astype(F32)
            d = d.astype(BF)
            slope[at, columns] = d
            ubias_o[0:1, columns] += jnp.sum(d.astype(F32), axis=0, keepdims=True)

    keep_d = pltpu.make_async_copy(slope, d_hidden_o, keep_sems.at[4])
    keep_d.start()

    def down_tile(i, target):
        f = pl.ds(pl.multiple_of(i * 256, 256), 256)
        for j in range(0, features, 1024):
            target[:, j : j + 1024] = general(act[:, f], gin[:, j : j + 1024], tn_dims).astype(BF)

    through(ff // 256, 256, features, down_tile, down_o)

    keep_normed.wait()
    keep_g.wait()
    keep_d.wait()
    for kind in range(2):
        own_row(kind).wait()
        for m in range(1, nz):
            other_row(kind, flip(z, m), m).wait_send()
            landed(kind, m).wait_recv()
    if gather:
        cots.drain()
        branch_over_y.wait()


def front(gather, split, rows, tokens, nz, many, features, att, ff, operands):
    hbm = pl.BlockSpec(memory_space=pl.ANY)
    vmem = pl.BlockSpec(memory_space=pltpu.VMEM)
    shares = (2, many, features // 4) if gather else (many, features)
    return pl.pallas_call(
        functools.partial(front_kernel, gather, split, rows, tokens),
        out_shape=[
            jax.ShapeDtypeStruct((many, features), BF),
            jax.ShapeDtypeStruct((many, features), BF),
            jax.ShapeDtypeStruct((4, nz * tokens, att), BF),
            jax.ShapeDtypeStruct((many, 128), F32),
            jax.ShapeDtypeStruct((ff, features), BF),
            jax.ShapeDtypeStruct((many, ff), BF),
            jax.ShapeDtypeStruct(shares, BF),
            jax.ShapeDtypeStruct((8, ff), F32),
            jax.ShapeDtypeStruct((ROT // 2, nz * tokens), F32),
            jax.ShapeDtypeStruct((ROT // 2, nz * tokens), F32),
            jax.ShapeDtypeStruct((8, nz * tokens), jnp.int32),
            jax.ShapeDtypeStruct((many // 2, features // 4), BF),
            jax.ShapeDtypeStruct((2, many, features // 4), BF),
        ],
        in_specs=[hbm, vmem, hbm, hbm, vmem, vmem, hbm, vmem, hbm, hbm, vmem, hbm],
        out_specs=[hbm, hbm, hbm, vmem, hbm, hbm, hbm, vmem, vmem, vmem, vmem, hbm, hbm],
        scratch_shapes=[
            pltpu.VMEM((many, features), BF),
            pltpu.VMEM((many, features), BF),
            pltpu.VMEM((3, features, att), BF),
            pltpu.VMEM((att, features), BF),
            pltpu.VMEM((features, ff), BF),
            pltpu.VMEM((ff, features), BF),
            pltpu.VMEM((nz, 4, tokens, att), BF),
            pltpu.VMEM((many, ff), BF),
            pltpu.VMEM((many, ff), BF),
            pltpu.VMEM((2, tokens, features), BF),
            pltpu.SemaphoreType.DMA((rows + 1, 2, 14)),
            pltpu.SemaphoreType.DMA((2, 2, 4)),
            pltpu.SemaphoreType.DMA((6,)),
            pltpu.SemaphoreType.DMA((5,)),
            pltpu.SemaphoreType.DMA((4,)),
            pltpu.SemaphoreType.DMA((2, 2 * many // tokens)),
            pltpu.SemaphoreType.DMA((2,)),
            pltpu.VMEM((2, rows, nz * tokens), jnp.int32),
            pltpu.SemaphoreType.DMA((3,)),
        ],
        compiler_params=pltpu.CompilerParams(
            collective_id=2, has_side_effects=True, vmem_limit_bytes=60 << 20
        ),
        cost_estimate=pl.CostEstimate(
            flops=2 * many * features * (6 * ff + 4 * att), bytes_accessed=100 << 20, transcendentals=0
        ),
        name="front",
    )(*operands)[:12]


def add_rows(target, one, two):
    @pl.loop(0, target.shape[0], step=32)
    def _(r):
        at = pl.ds(pl.multiple_of(r, 32), 32)
        target[at] = (one[at].astype(F32) + two[at].astype(F32)).astype(BF)


class Chain:
    COLUMNS = 256
    SLOTS = {"own": 3, "in": 2, "cross": 2, "sum": 4, "total": 6}
    END_LAG = 5
    MID_LAG = 2
    INWARD = 2
    APART = 3
    ASIDE = 8

    @classmethod
    def layout(cls, arrays):
        chunks, rings = [], {}
        for a, (rows, columns, size, _) in enumerate(arrays):
            size, wide = math.gcd(rows, size), math.gcd(columns, cls.COLUMNS)
            rings[wide] = max(rings.get(wide, 0), size)
            chunks += [(a, r, size, c, wide) for r in range(0, rows, size) for c in range(0, columns, wide)]
        return chunks, rings

    @classmethod
    def scratch(cls, arrays):
        chunks, rings = cls.layout(arrays)
        return [pltpu.VMEM((k, rows, wide), BF) for wide, rows in rings.items() for k in cls.SLOTS.values()] + [
            pltpu.SemaphoreType.DMA((8, len(chunks))),
            pltpu.SemaphoreType.DMA((3, 3)),
            pltpu.SemaphoreType.DMA((len(chunks),)),
        ]

    def __init__(self, arrays, own, outs, landed, crossed, scratch):
        self.arrays, self.own, self.outs, self.landed, self.crossed = arrays, own, outs, landed, crossed
        self.chunks, rings = self.layout(arrays)
        scratch = list(scratch)
        self.rings = {wide: {name: scratch.pop(0) for name in self.SLOTS} for wide in rings}
        self.sems, self.load_sems, self.keep_sem = scratch
        self.n = len(self.chunks)
        self.x, self.z = lax.axis_index("dp"), lax.axis_index("blk")
        self.at_end = (self.z == 0) | (self.z == 3)
        self.inner = jnp.where(self.z == 0, 1, 2)
        self.outer = jnp.where(self.z == 1, 0, 3)

    def send(self, kind, c, src, dst, device):
        return pltpu.make_async_remote_copy(
            src, dst, self.sems.at[2 * kind, c], self.sems.at[2 * kind + 1, c],
            device_id=device, device_id_type=MESH,
        )

    def part(self, refs, c):
        a, r, rows, column, columns = self.chunks[c]
        return refs[a].at[pl.ds(r, rows), pl.ds(column, columns)]

    def final(self, c, half):
        a, r, rows, column, columns = self.chunks[c]
        return self.outs[a].at[half, pl.ds(r, rows), pl.ds(column, columns)]

    def slot(self, name, c):
        _, _, rows, _, columns = self.chunks[c]
        return self.rings[columns][name].at[c % self.SLOTS[name], pl.ds(0, rows)]

    def go_in(self, c):
        return self.send(0, c, self.part(self.own, c), self.part(self.landed, c), {"blk": self.inner})

    def arrive_in(self, c):
        ref = self.part(self.landed, c)
        return self.send(0, c, ref, ref, {"blk": self.outer})

    def go_mid(self, c):
        return self.send(1, c, self.slot("sum", c), self.part(self.crossed, c), {"blk": 3 - self.z})

    def go_out(self, c):
        return self.send(2, c, self.slot("total", c), self.final(c, self.x), {"blk": self.outer})

    def arrive_out(self, c):
        return self.send(2, c, self.final(c, self.x), self.final(c, self.x), {"blk": self.inner})

    def go_x(self, c, end):
        src = self.final(c, self.x) if end else self.slot("total", c)
        return self.send(3, c, src, self.final(c, self.x), {"dp": 1 - self.x})

    def arrive_x(self, c):
        ref = self.final(c, 1 - self.x)
        return self.send(3, c, ref, ref, {"dp": 1 - self.x})

    def load(self, name, refs, c):
        at = self.load_sems.at[list(self.SLOTS).index(name), c % self.SLOTS[name]]
        return pltpu.make_async_copy(self.part(refs, c), self.slot(name, c), at)

    def load_own(self, c):
        return self.load("own", self.own, c)

    def first_of(self, array):
        return [a for a, *_ in self.chunks].index(array)

    def in_hbm(self, c):
        return c < self.n and self.arrays[self.chunks[c][0]][3]

    def keep(self, c):
        return pltpu.make_async_copy(self.slot("total", c), self.final(c, self.x), self.keep_sem.at[c])

    @property
    def steps(self):
        return self.n + self.END_LAG

    def begin(self):
        @pl.when(self.at_end)
        def _():
            for c in range(min(self.INWARD, self.n)):
                self.go_in(c).start()

        @pl.when(jnp.logical_not(self.at_end))
        def _():
            for c in range(2):
                if self.in_hbm(c):
                    self.load_own(c).start()

    def sent(self, c):
        self.go_out(c).wait_send()
        if c < self.n - self.APART:
            self.go_x(c, False).wait_send()
        self.keep(c).wait()

    def step(self, c):
        n, slots = self.n, self.SLOTS

        @pl.when(self.at_end)
        def _():
            if c < n:
                self.go_in(c).wait_send()
                if c + self.INWARD < n:
                    self.go_in(c + self.INWARD).start()
            d = c - self.END_LAG
            if 0 <= d < n:
                self.arrive_out(d).wait_recv()
                if d >= self.ASIDE:
                    self.go_x(d - self.ASIDE, True).wait_send()
                if d < n - self.APART:
                    self.go_x(d, True).start()

        if c >= n + self.MID_LAG:
            return

        @pl.when(jnp.logical_not(self.at_end))
        def _():
            d = c - self.MID_LAG
            crossing = 0 <= d < n
            if c < n:
                if self.in_hbm(c + 2):
                    self.load_own(c + 2).start()
                self.arrive_in(c).wait_recv()
                self.load("in", self.landed, c).start()
            if crossing:
                self.go_mid(d).wait_recv()
                self.load("cross", self.crossed, d).start()
            if c < n:
                if self.in_hbm(c):
                    self.load_own(c).wait()
                    mine = self.slot("own", c)
                else:
                    mine = self.part(self.own, c)
                if c >= slots["sum"]:
                    self.go_mid(c - slots["sum"]).wait_send()
                self.load("in", self.landed, c).wait()
                add_rows(self.slot("sum", c), self.slot("in", c), mine)
                self.go_mid(c).start()
            if crossing:
                if d >= slots["total"]:
                    self.sent(d - slots["total"])
                self.load("cross", self.crossed, d).wait()
                add_rows(self.slot("total", d), self.slot("cross", d), self.slot("sum", d))
                self.go_out(d).start()
                if d < n - self.APART:
                    self.go_x(d, False).start()
                self.keep(d).start()

    def finish(self):
        n, slots = self.n, self.SLOTS

        @pl.when(self.at_end)
        def _():
            for c in range(max(0, n - self.ASIDE), n - self.APART):
                self.go_x(c, True).wait_send()

        @pl.when(jnp.logical_not(self.at_end))
        def _():
            for c in range(max(0, n - slots["sum"]), n):
                self.go_mid(c).wait_send()
            for c in range(max(0, n - slots["total"]), n):
                self.sent(c)

        for c in range(n - self.APART):
            self.arrive_x(c).wait_recv()


def greet(devices):
    barrier = pltpu.get_barrier_semaphore()
    for device in devices:
        pl.semaphore_signal(barrier, inc=1, device_id=device, device_id_type=MESH)
    pl.semaphore_wait(barrier, len(devices))


def turn(source, cos_t, sin_t):
    half = ROT // 2
    front_half, back_half = source[:half], source[half:ROT]
    return jnp.concatenate(
        [front_half * cos_t - back_half * sin_t, back_half * cos_t + front_half * sin_t, source[ROT:]], axis=0
    )


def attention_heads(
    first_head, heads, tile, land, cos_ref, sin_ref, start_ref, out, q_t, k_t, v_t, g_t, q_n, k_n, probs, dk_acc, dv_acc,
    between,
):
    total = land.shape[1]
    steps = total // tile
    scale = HD**-0.5
    hs = range(heads)

    def lanes(h):
        return slice((first_head + h) * HD, (first_head + h + 1) * HD)

    @pl.loop(0, steps)
    def _(i):
        place = pl.ds(pl.multiple_of(i * tile, tile), tile)
        cos_t, sin_t = cos_ref[:, place], sin_ref[:, place]
        for h in hs:
            x = turn(land[0, place, lanes(h)].astype(F32).T, cos_t, sin_t) * scale
            q_t[h, :, place] = x.astype(BF)
            q_n[h, place, :] = x.T.astype(BF)
            x = turn(land[1, place, lanes(h)].astype(F32).T, cos_t, sin_t)
            k_t[h, :, place] = x.astype(BF)
            k_n[h, place, :] = x.T.astype(BF)
            v_t[h, :, place] = land[2, place, lanes(h)].astype(F32).T.astype(BF)
            g_t[h, :, place] = land[3, place, lanes(h)].astype(F32).T.astype(BF)
            dk_acc[h, place, :] = jnp.zeros((tile, HD), F32)
            dv_acc[h, place, :] = jnp.zeros((tile, HD), F32)

    def one_tile(i):
        qs = pl.ds(pl.multiple_of(i * tile, tile), tile)
        start = start_ref[0:1, qs]
        queries = [q_t[h, :, qs] for h in hs]
        queries_n = [q_n[h, qs, :] for h in hs]
        cots = [g_t[h, :, qs] for h in hs]
        cots_n = [land[3, qs, lanes(h)] for h in hs]
        key_at = lax.broadcasted_iota(jnp.int32, (tile, tile), 0)
        query_at = lax.broadcasted_iota(jnp.int32, (tile, tile), 1)

        def score(j, tops, diagonal):
            first = pl.multiple_of(j * tile, tile)
            allowed = key_at >= (start - first)
            if diagonal:
                allowed = allowed & (key_at <= query_at)
            result = []
            for h in hs:
                s = dot32(k_n[h, pl.ds(first, tile), :], queries[h])
                s = jnp.where(allowed, s, NEGATIVE)
                probs[h, pl.ds(first, tile), :] = s
                result.append(jnp.maximum(tops[h], jnp.max(s, axis=0, keepdims=True)))
            return tuple(result)

        tops = tuple(jnp.full((1, tile), NEGATIVE, F32) for _ in hs)
        tops = lax.fori_loop(0, i, lambda j, c: score(j, c, False), tops)
        tops = score(i, tops, True)

        def mix(j, carry):
            sums, mixed = carry
            ks = pl.ds(pl.multiple_of(j * tile, tile), tile)
            new_sums, new_mixed = [], []
            for h in hs:
                p = jnp.exp(probs[h, ks, :] - tops[h])
                probs[h, ks, :] = p
                new_sums.append(sums[h] + jnp.sum(p, axis=0, keepdims=True))
                new_mixed.append(mixed[h] + dot32(v_t[h, :, ks], p.astype(BF)))
            return tuple(new_sums), tuple(new_mixed)

        zeros = tuple(jnp.zeros((1, tile), F32) for _ in hs)
        wide_zeros = tuple(jnp.zeros((HD, tile), F32) for _ in hs)
        sums, mixed = lax.fori_loop(0, i + 1, mix, (zeros, wide_zeros))
        inverse = [1.0 / sums[h] for h in hs]
        mixed = [mixed[h] * inverse[h] for h in hs]
        delta = [jnp.sum(mixed[h] * cots[h].astype(F32), axis=0, keepdims=True) for h in hs]

        def back(j, carry):
            ks = pl.ds(pl.multiple_of(j * tile, tile), tile)
            result = []
            for h in hs:
                p = probs[h, ks, :] * inverse[h]
                dp = dot32(land[2, ks, lanes(h)], cots[h])
                ds = (p * (dp - delta[h])).astype(BF)
                dv_acc[h, ks, :] += dot32(p.astype(BF), cots_n[h])
                dk_acc[h, ks, :] += dot32(ds, queries_n[h])
                result.append(carry[h] + dot32(k_t[h, :, ks], ds))
            return tuple(result)

        dq = lax.fori_loop(0, i + 1, back, wide_zeros)
        cos_t, sin_t = cos_ref[:, qs], sin_ref[:, qs]
        for h in hs:
            out[i, 0, :, lanes(h)] = turn(dq[h] * scale, cos_t, -sin_t).T.astype(BF)
            out[i, 3, :, lanes(h)] = mixed[h].T.astype(BF)

    @pl.loop(0, steps)
    def _(i):
        one_tile(i)
        between(i)

    @pl.loop(0, steps)
    def _(i):
        place = pl.ds(pl.multiple_of(i * tile, tile), tile)
        cos_t, sin_t = cos_ref[:, place], sin_ref[:, place]
        for h in hs:
            out[i, 1, :, lanes(h)] = turn(dk_acc[h, place, :].T, cos_t, -sin_t).T.astype(BF)
            out[i, 2, :, lanes(h)] = dv_acc[h, place, :].astype(BF)


def back_kernel(
    arrays, scatter, split, heads, tokens, land_ref, cos_ref, sin_ref, start_ref, g_ref, normed_ref, wq_ref, wo_ref,
    branch_ff, branch_y, d_hidden_ref, wu_ref, input_ref, grad_ref, stats_ref, gain_ref, out_bias_ref, down_bias_ref,
    ubias_ref, *refs,
):
    x, z, t = lax.axis_index("dp"), lax.axis_index("blk"), lax.axis_index("tensor")
    refs = list(refs)

    def take_refs(n):
        taken = refs[:n]
        del refs[:n]
        return taken

    own = take_refs(1)
    (home,) = take_refs(1)
    outs, landed, crossed = take_refs(4), take_refs(4), take_refs(4)
    up_part, dnorm_ff = take_refs(2)
    home_x, branch_y2, dnorm_y, sum_ff, over_x_ff, cross_ff = take_refs(6) if scatter else [None] * 6
    output_o, input_grad_o, small = take_refs(3) if scatter else [None] * 3
    out, dwo, dwq, load_sems, home_sems, home_keep, stage_sems = take_refs(7)
    give, take, take_y, tile_sems, scatter_sems, cross_sems = take_refs(6) if scatter else [None] * 6
    d_normed, moments, stats, small_in, norm_sems = take_refs(5) if scatter else [None] * 5
    nz, _, _, att = out.shape
    total = nz * tokens
    many, features = normed_ref.shape
    half, width = many // 2, features // 4
    rows = nz // 2
    groups = att // (heads * HD)
    peers = {"x": {"dp": 1 - x}, "y": {"tensor": flip(t, 2)}, "c": {"tensor": flip(t, 1)}}
    greet([{"blk": flip(z, m)} for m in range(1, nz)] + (list(peers.values()) if scatter else [peers["x"]]))
    work = Chain(arrays, own + [up_part, dwo, dwq], outs, landed, crossed, refs)
    work.begin()

    def remote(which, stage, src, dst, to):
        return pltpu.make_async_remote_copy(
            src, dst, scatter_sems.at[0, which, stage], scatter_sems.at[1, which, stage],
            device_id=peers[to], device_id_type=MESH,
        )

    if scatter:
        small[...] = jnp.zeros_like(small)
        ff = ubias_ref.shape[1]
        for r in range(ff // width):
            small[pl.ds(3 + x * (ff // width) + r, 1), :] = ubias_ref[0:1, r * width : (r + 1) * width]
        qkv_row = 3 + 2 * ff // width

    def branch_over_y():
        return remote(0, 0, branch_ff.at[1 - t // 2, pl.ds(half, half)], branch_y2, "y")

    def dnorm_over_y():
        return remote(1, 0, dnorm_ff.at[1 - t // 2], dnorm_y, "y")

    def ff_x(which):
        return remote(which, 1, sum_ff.at[which, pl.ds((1 - x) * half, half)], over_x_ff.at[which], "x")

    def add_ff(which):
        (dnorm_over_y if which else branch_over_y)().wait_recv()
        ours = (branch_ff, dnorm_ff)[which]
        size = half // 4

        def at(k):
            return pl.ds(k * size, size)

        def tile(i, k):
            n = 2 * i + k % 2
            return give.at[n // 4, at(n % 4)]

        def theirs(k):
            if which == 1:
                return dnorm_y.at[at(k)]
            return branch_y.at[at(k)] if k < 4 else branch_y2.at[at(k - 4)]

        def fetch(k):
            return [
                pltpu.make_async_copy(ours.at[t // 2, at(k)], tile(0, k), tile_sems.at[0, k % 2]),
                pltpu.make_async_copy(theirs(k), tile(1, k), tile_sems.at[1, k % 2]),
            ]

        def keep(k):
            return pltpu.make_async_copy(tile(2, k), sum_ff.at[which, at(k)], tile_sems.at[2, k % 2])

        blocks = many // size
        for copy in fetch(0):
            copy.start()
        for k in range(blocks):
            if k + 1 < blocks:
                for copy in fetch(k + 1):
                    copy.start()
            for copy in fetch(k):
                copy.wait()
            if k >= 2:
                keep(k - 2).wait()
            add_rows(tile(2, k), tile(0, k), tile(1, k))
            keep(k).start()
        for k in range(blocks - 2, blocks):
            keep(k).wait()
        ff_x(which).start()

    tn_dims = (((0,), (0,)), ((), ()))
    nt_dims = (((1,), (1,)), ((), ()))
    general = functools.partial(lax.dot_general, preferred_element_type=F32)
    at_step, ready = [0], [work.first_of(2)]

    def step():
        work.step(at_step[0])
        assert at_step[0] + work.INWARD < ready[0]
        at_step[0] += 1

    def spread(d_hidden, weight, normed, stage):
        ff = d_hidden.shape[1]
        part = features // 2
        wide = pl.ds(pl.multiple_of(x * ff, 128), ff)
        loads = [
            pltpu.make_async_copy(d_hidden_ref, d_hidden, load_sems.at[0, 0]),
            pltpu.make_async_copy(wu_ref.at[:, wide] if split else wu_ref, weight, load_sems.at[0, 1]),
        ] + [
            pltpu.make_async_copy(normed_ref.at[:, pl.ds(k * part, part)], normed.at[k], load_sems.at[1, k]) for k in range(2)
        ]
        for copy in loads:
            copy.start()
        loads[0].wait()
        loads[1].wait()

        def value(at, columns):
            return general(d_hidden[at, :], weight[columns, :], nt_dims)

        if scatter:
            core_share(cross_ff, stage, cross_sems, stage_sems, tokens, t, value, dnorm_ff, step)
            dnorm_over_y().start()
        else:
            for r in range(nz):
                at = pl.ds(r * tokens, tokens)
                for columns in range(0, features, 512):
                    stage[0, :, columns : columns + 512] = value(at, pl.ds(columns, 512)).astype(BF)
                copy = pltpu.make_async_copy(stage.at[0], dnorm_ff.at[at], stage_sems.at[0])
                copy.start()
                copy.wait()
        step()

        def keep(k, i):
            rows = pl.ds(pl.multiple_of(k * part + i * 256, 256), 256)
            return pltpu.make_async_copy(
                stage.at[i % 2, pl.ds(0, 256), pl.ds(0, ff)], up_part.at[rows], stage_sems.at[i % 2]
            )

        for k in range(2):
            loads[2 + k].wait()

            @pl.loop(0, part // 256)
            def _(i, k=k):
                @pl.when(i >= 2)
                def _():
                    keep(k, i - 2).wait()

                f = pl.ds(pl.multiple_of(i * 256, 256), 256)
                stage[i % 2, :256, :ff] = general(normed[k, :, f], d_hidden[...], tn_dims).astype(BF)
                keep(k, i).start()

            for i in range(part // 256 - 2, part // 256):
                keep(k, i).wait()
            step()

    if scatter:
        branch_over_y().start()
    pl.run_scoped(
        spread,
        pltpu.VMEM(d_hidden_ref.shape, BF),
        pltpu.VMEM((features, d_hidden_ref.shape[1]), BF),
        pltpu.VMEM((2, many, features // 2), BF),
        pltpu.VMEM((2, tokens, features), BF),
    )

    def lanes(p):
        return pl.ds(p * heads * HD, heads * HD)

    def home_copy(p, m, src, dst):
        return pltpu.make_async_remote_copy(
            src, dst, home_sems.at[0, p, m], home_sems.at[1, p, m], device_id={"blk": flip(z, m)}, device_id_type=MESH
        )

    def go_home(p, m):
        src = out.at[flip(z, m), :, :, lanes(p)]
        dst = home.at[:, z, :, lanes(p)]
        if m == 0:
            return pltpu.make_async_copy(src, dst, home_keep.at[p])
        return home_copy(p, m, src, dst)

    def arrive_home(p, m):
        ref = home.at[:, flip(z, m), :, lanes(p)]
        return home_copy(p, m, ref, ref)

    def attend(land, *scratch):
        load = pltpu.make_async_copy(land_ref, land, load_sems.at[0, 0])
        load.start()
        load.wait()
        for p in range(groups):
            plan = SCHEDULE[p] if p < len(SCHEDULE) else ()
            first = at_step[0]
            at_step[0] += sum(plan)

            def between(i, plan=plan, first=first):
                at = first
                for tile, steps in enumerate(plan):
                    if steps:

                        @pl.when(i == tile)
                        def _(at=at, steps=steps):
                            for c in range(at, at + steps):
                                work.step(c)

                    at += steps

            attention_heads(p * heads, heads, tokens, land, cos_ref, sin_ref, start_ref, out, *scratch, between)
            for m in (2, 3, 1, 0):
                go_home(p, m).start()
            if scatter:
                for which in (0, 1) if groups == 1 else (p,):
                    add_ff(which)

    pl.run_scoped(
        attend,
        pltpu.VMEM((4, total, att), BF),
        *[pltpu.VMEM((heads, HD, total), BF)] * 4,
        *[pltpu.VMEM((heads, total, HD), BF)] * 2,
        pltpu.VMEM((heads, total, tokens), F32),
        *[pltpu.VMEM((heads, total, HD), F32)] * 2,
    )
    def share_home(p):
        src, dst = home.at[:, pl.ds((1 - x) * rows, rows), :, lanes(p)], home_x.at[:, :, :, lanes(p)]
        return remote(p, 2, src, dst, "x")

    def come_home(p):
        for m in range(nz):
            if m == 0:
                go_home(p, m).wait()
            else:
                go_home(p, m).wait_send()
                arrive_home(p, m).wait_recv()
        if scatter:
            share_home(p).start()

    last = work.first_of(2) - work.INWARD - 2
    assert at_step[0] <= last - HOME_APART * (groups - 1)
    while at_step[0] <= last:
        for p in range(groups):
            if at_step[0] == last - HOME_APART * (groups - 1 - p):
                come_home(p)
        step()

    def over_core(which):
        return remote(which, 3, give, take.at[which], "c")

    def over_y(which):
        return remote(which, 4, take.at[which, 1 - t // 2], take_y.at[which], "y")

    def project(stream, hcat, hx, wcat, wo):
        def piece(i, r):
            at = pl.ds(r * tokens, tokens)
            return hcat.at[at, pl.ds(i * att, att)] if split else hcat.at[i, at]

        loads = [
            pltpu.make_async_copy(home.at[i, r], piece(i, r), load_sems.at[i, r])
            for i in (3, 0, 1, 2)
            for r in range(nz)
        ]
        weights = [] if not scatter else [
            pltpu.make_async_copy(
                wq_ref.at[i, :, pl.ds(pl.multiple_of(side * att, 128), att)],
                wcat.at[s, :, pl.ds(i * att, att)],
                load_sems.at[4 + s, i],
            )
            for s, side in enumerate((x, 1 - x))
            for i in range(3)
        ] + [
            pltpu.make_async_copy(wo_ref.at[pl.ds(side * att, att)], wo.at[s], load_sems.at[4 + s, 3])
            for s, side in enumerate((x, 1 - x))
        ]
        part = features // 2

        def streamed(k):
            source = g_ref if k < 2 else normed_ref
            return pltpu.make_async_copy(source.at[:, pl.ds((k % 2) * part, part)], stream.at[k % 2], load_sems.at[6, k % 2])

        for copy in loads[:4] + [streamed(0), streamed(1)] + loads[4:] + (weights if scatter else []):
            copy.start()
        step()
        for copy in loads:
            copy.wait()
        if split:
            attended = hcat[:, 3 * att :]
        else:
            d_qkv, attended = jnp.concatenate([hcat[i] for i in range(3)], axis=1), hcat[3]
        for k in range(2):
            streamed(k).wait()
            for j in range(part // width):
                value = general(attended, stream[k, :, j * width : (j + 1) * width], tn_dims)
                dwo[pl.ds((k * (part // width) + j) * att, att), :] = value.astype(BF)
            streamed(k + 2).start()
        ready[0] = work.first_of(3)
        for k in range(2):
            step()
            streamed(k + 2).wait()

            @pl.loop(0, part // 256)
            def _(j, k=k):
                f = pl.ds(pl.multiple_of(j * 256, 256), 256)
                value = general(stream[k, :, f], hcat[:, : 3 * att] if split else d_qkv, tn_dims).astype(BF)
                for i in range(3):
                    at = pl.multiple_of(i * features + k * part + j * 256, 256)
                    dwq[pl.ds(at, 256), :] = value[:, i * att : (i + 1) * att]

        ready[0] = work.n + work.steps
        if not scatter:
            return
        others = [
            pltpu.make_async_copy(
                home_x.at[i, r], hx.at[pl.ds(r * tokens, tokens), pl.ds(i * att, att)], load_sems.at[i, r]
            )
            for i in range(4)
            for r in range(rows)
        ]
        for p in range(groups):
            share_home(p).wait_recv()
        for copy in others:
            copy.start()
        for copy in weights + others:
            copy.wait()

        def share(which, of_core, target, plus):
            @pl.loop(0, 2 * rows)
            def _(k):
                v = k // rows
                columns = pl.ds(pl.multiple_of((2 * v + of_core) * width, width), width)
                at = pl.ds(pl.multiple_of((k % rows) * tokens, tokens), tokens)
                mine = pl.ds(pl.multiple_of(x * half + (k % rows) * tokens, tokens), tokens)
                if which == 0:
                    value = dot32(hcat[mine, 3 * att :], wo[0, :, columns]) + dot32(hx[at, 3 * att :], wo[1, :, columns])
                else:
                    value = general(hcat[mine, : 3 * att], wcat[0, columns, :], nt_dims)
                    value = value + general(hx[at, : 3 * att], wcat[1, columns, :], nt_dims)
                if plus:
                    value = value + target[v, at, :].astype(F32)
                target[v, at, :] = value.astype(BF)

        sums = jnp.sum(hcat[:, : 3 * att].astype(F32), axis=0, keepdims=True)
        for i in range(3):
            at = pl.ds(pl.multiple_of(x * att, 128), att)
            small[qkv_row + i : qkv_row + i + 1, at] = sums[:, i * att : (i + 1) * att]
        core = t % 2
        share(0, 1 - core, give, False)
        over_core(0).start()
        step()
        over_core(0).wait_send()
        share(1, 1 - core, give, False)
        over_core(1).start()
        step()
        for which in range(2):
            over_core(which).wait_recv()
            share(which, core, take.at[which], True)
            over_y(which).start()
            step()

    pl.run_scoped(
        project,
        pltpu.VMEM((2, many, features // 2), BF),
        pltpu.VMEM((many, 4 * att) if split else (4, many, att), BF),
        pltpu.VMEM((half, 4 * att), BF),
        pltpu.VMEM((2, features, 3 * att), BF),
        pltpu.VMEM((2, att, features), BF),
    )

    def load_to(refs):
        copies = [pltpu.make_async_copy(src, dst, tile_sems.at[i // 2, i % 2]) for i, (src, dst) in enumerate(refs)]
        for copy in copies:
            copy.start()
        for copy in copies:
            copy.wait()

    mine = pl.ds(x * half, half)
    spare = 1 - t // 2

    def total_share(which):
        over_y(which).wait_recv()
        over_y(which).wait_send()
        ff_x(which).wait_recv()
        load_to(
            [
                (sum_ff.at[which, mine], give.at[0]),
                (over_x_ff.at[which], give.at[1]),
                ((input_ref, grad_ref)[which], take.at[which, spare]),
            ]
            + ([(stats_ref.at[mine], stats)] if which else [])
        )

        def value(at):
            ff = give[0, at, :].astype(F32) + give[1, at, :].astype(F32)
            return ff + (take[which, t // 2, at, :].astype(F32) + take_y[which, at, :].astype(F32))

        return value

    def block_at(i):
        return pl.ds(pl.multiple_of(i * 128, 128), 128)

    def save(which):
        return pltpu.make_async_copy(take_y.at[which], (output_o, input_grad_o)[which], home_keep.at[which])

    def norm_copy(k, src, dst, device):
        return pltpu.make_async_remote_copy(
            src, dst, norm_sems.at[0, k], norm_sems.at[1, k], device_id=device, device_id_type=MESH
        )

    def exchange(k):
        return norm_copy(k, moments.at[2 * k], moments.at[2 * k + 1], peers["cy"[k]])

    def output():
        over_core(1).wait_send()
        value = total_share(0)

        @pl.loop(0, half // 128)
        def _(i):
            at = block_at(i)
            total = take[0, spare, at, :].astype(F32) + (value(at) + out_bias_ref[...] + down_bias_ref[...])
            take_y[0, at, :] = total.astype(BF)

        save(0).start()

    def own_gain():
        return gain_ref[:, pl.ds(pl.multiple_of(t * width, width), width)]

    def standardized(at):
        inverse = stats[at, 64:65]
        return (take[0, spare, at, :].astype(F32) - stats[at, 0:1]) * inverse, inverse

    def norm_sums():
        value = total_share(1)

        @pl.loop(0, half // 128)
        def _(i):
            at = block_at(i)
            d = value(at)
            d_normed[at, :] = d
            xhat, _ = standardized(at)
            scaled = d * own_gain()
            one = jnp.sum(scaled, axis=-1, keepdims=True)
            two = jnp.sum(scaled * xhat, axis=-1, keepdims=True)
            lane = lax.broadcasted_iota(jnp.int32, (128, 128), 1)
            moments[0, at, :] = jnp.where(lane < 64, one, two)
            small[0:1, :] += jnp.sum(d * xhat, axis=0, keepdims=True)
            small[1:2, :] += jnp.sum(d, axis=0, keepdims=True)
            small[2:3, :] += jnp.sum(take[1, spare, at, :].astype(F32), axis=0, keepdims=True)

        exchange(0).start()

    def norm_sums_core():
        exchange(0).wait()
        moments[2] = moments[0] + moments[1]
        exchange(1).start()

    def norm_back():
        exchange(1).wait()

        @pl.loop(0, half // 128)
        def _(i):
            at = block_at(i)
            total = (moments[2, at, :] + moments[3, at, :]) * (1.0 / features)
            xhat, inverse = standardized(at)
            scaled = d_normed[at, :] * own_gain()
            back = inverse * (scaled - total[:, 0:1] - xhat * total[:, 64:65])
            take_y[1, at, :] = (take[1, spare, at, :].astype(F32) + back).astype(BF)

        save(1).start()

    def small_sums(k):
        device = ({"dp": 1 - x}, {"blk": flip(z, 1)}, {"blk": flip(z, 2)})[k]
        copy = norm_copy(2 + k, small, small_in.at[k], device)
        copy.start()
        copy.wait()
        small[...] += small_in[k]

    stages = {
        "output": output, "norm_sums": norm_sums, "norm_sums_core": norm_sums_core, "norm_back": norm_back,
        "dp": functools.partial(small_sums, 0), "blk_1": functools.partial(small_sums, 1),
        "blk_2": functools.partial(small_sums, 2),
    }
    later = dict(LATER) if scatter else {}
    while at_step[0] < work.steps:
        for name in later.pop(at_step[0], ()):
            stages[name]()
        step()
    assert not later
    work.finish()
    if scatter:
        for which in range(2):
            ff_x(which).wait_send()
            save(which).wait()
        branch_over_y().wait_send()
        dnorm_over_y().wait_send()
        for p in range(groups):
            share_home(p).wait_send()


def weight_arrays(down, d_hidden, features, att):
    return [
        (*down, 1024, True), (features, d_hidden[1], 1024, True), (4 * att, features // 4, 1024, False),
        (3 * features, att, 512, False),
    ]


def back(
    scatter, split, tokens, land, cos_t, sin_t, start, cotangent, normed, wq, wo, branch_ff, branch_y, d_hidden, wu, down,
    block_input, grad_output, stats, gain, out_bias, down_bias, up_bias_part,
):
    _, total, att = land.shape
    nz = total // tokens
    many, features = normed.shape
    width, half = features // 4, many // 2
    heads = min(2, att // HD)
    groups = att // (heads * HD)
    ff = d_hidden.shape[1]
    arrays = weight_arrays(down.shape, d_hidden.shape, features, att)
    shapes = [a[:2] for a in arrays]
    hbm = pl.BlockSpec(memory_space=pl.ANY)
    vmem = pl.BlockSpec(memory_space=pltpu.VMEM)
    dma = pltpu.SemaphoreType.DMA
    scatter_scratch = [
        pltpu.VMEM((2, half, width), BF),
        pltpu.VMEM((2, 2, half, width), BF),
        pltpu.VMEM((2, half, width), BF),
        dma((3, 2)),
        dma((2, 2, 5)),
        dma((2, 2 * many // tokens)),
        pltpu.VMEM((half, width), F32),
        pltpu.VMEM((4, half, 128), F32),
        pltpu.VMEM((half, 128), F32),
        pltpu.VMEM((3, 16, width), F32),
        dma((2, 5)),
    ]
    scatter_outs = [
        jax.ShapeDtypeStruct((4, nz // 2, tokens, att), BF),
        jax.ShapeDtypeStruct((half, width), BF),
        jax.ShapeDtypeStruct((many, width), BF),
        jax.ShapeDtypeStruct((2, many, width), BF),
        jax.ShapeDtypeStruct((2, half, width), BF),
        jax.ShapeDtypeStruct((2, many, width), BF),
        jax.ShapeDtypeStruct((half, width), BF),
        jax.ShapeDtypeStruct((half, width), BF),
        jax.ShapeDtypeStruct((16, width), F32),
    ]
    results = pl.pallas_call(
        functools.partial(back_kernel, arrays, scatter, split, heads, tokens),
        out_shape=[jax.ShapeDtypeStruct((4, nz, tokens, att), BF)]
        + [jax.ShapeDtypeStruct((2,) + s, BF) for s in shapes]
        + [jax.ShapeDtypeStruct(s, BF) for s in shapes] * 2
        + [jax.ShapeDtypeStruct((features, ff), BF)]
        + [jax.ShapeDtypeStruct((2, many, width) if scatter else (many, features), BF)]
        + (scatter_outs if scatter else []),
        in_specs=[hbm] + [vmem] * 3 + [hbm] * 8 + [hbm] * 3 + [vmem] * 4 + [hbm],
        out_specs=[hbm] * 15 + ([hbm] * 8 + [vmem] if scatter else []),
        scratch_shapes=[
            pltpu.VMEM((nz, 4, tokens, att), BF),
            pltpu.VMEM(shapes[2], BF),
            pltpu.VMEM(shapes[3], BF),
            dma((7, 4)),
            dma((2, groups, nz)),
            dma((max(groups, 2),)),
            dma((4,)),
        ]
        + (scatter_scratch if scatter else [])
        + Chain.scratch(arrays),
        compiler_params=pltpu.CompilerParams(collective_id=3, has_side_effects=True, vmem_limit_bytes=60 << 20),
        cost_estimate=pl.CostEstimate(
            flops=12 * (att // HD) * total * total * HD * 4, bytes_accessed=1 << 29, transcendentals=0
        ),
        name="back",
    )(land, cos_t, sin_t, start, cotangent, normed, wq, wo, branch_ff, branch_y, d_hidden, wu, block_input, grad_output, stats,
      gain, out_bias, down_bias, up_bias_part, down)
    return results[0], results[1:5], results[14], results[21:]


def widen(source, out_shape, block, in_map, out_map, grid):
    def body(source_ref, out_ref):
        out_ref[...] = source_ref[0].astype(F32)

    return pl.pallas_call(
        body,
        out_shape=jax.ShapeDtypeStruct(out_shape, F32),
        grid=grid,
        in_specs=[pl.BlockSpec((1,) + block, in_map)],
        out_specs=pl.BlockSpec(block, out_map),
        compiler_params=pltpu.CompilerParams(vmem_limit_bytes=32 << 20),
        cost_estimate=pl.CostEstimate(flops=0, bytes_accessed=source.size * 6, transcendentals=0),
        name="widen",
    )(source)


def widen_rows(source):
    _, rows, columns = source.shape
    size = min(rows, (1 << 18) // columns)
    steps = rows // size
    return widen(
        source, (2 * rows, columns), (size, columns), lambda i, h: (h, i, 0), lambda i, h: (h * steps + i, 0), (steps, 2)
    )


def widen_columns(source):
    _, rows, columns = source.shape
    if columns % 128:
        return jnp.concatenate([source[0], source[1]], axis=1).astype(F32)
    size = min(rows, (1 << 18) // columns)
    return widen(
        source, (rows, 2 * columns), (size, columns), lambda i, h: (h, i, 0), lambda i, h: (i, h), (rows // size, 2)
    )


def widen_blocks(source):
    _, rows, columns = source.shape
    rows = rows // 4
    return widen(
        source, (2 * rows, 4 * columns), (rows, columns), lambda h, j: (h, j, 0), lambda h, j: (h, j), (2, 4)
    )


def scatter_sum(share):
    whole = lax.psum_scatter(share.astype(BF), "dp", scatter_dimension=0, tiled=True)
    return lax.psum_scatter(whole, "tensor", scatter_dimension=2, tiled=True).astype(F32)


def butterfly(value, axes):
    for axis, size in axes:
        mask = 1
        while mask < size:
            value = value + swap(value, axis, size, mask)
            mask *= 2
    return value


SCHEDULE = ((0, 1, 1, 1), (0, 1, 0, 1))
HOME_APART = 2
LATER = {26: ["output"], 28: ["norm_sums"], 29: ["norm_sums_core"], 31: ["norm_back"], 32: ["dp"], 33: ["blk_1"], 34: ["blk_2"]}


def local(
    nx, nz, nt, block_input, segment_ids, layer_norm_gain, layer_norm_bias, qkv_weight, qkv_bias, out_weight, out_bias,
    up_weight, up_bias, down_weight, down_bias, grad_output,
):
    rows, tokens, width = block_input.shape
    all_rows = nx * rows
    features = nt * width
    many = all_rows * tokens
    x, z, t = lax.axis_index("dp"), lax.axis_index("blk"), lax.axis_index("tensor")
    att = qkv_weight.shape[2] // nx
    ff = up_weight.shape[1] // nx

    split = att % 128 == 0
    gather = nt == 4 and nx == 2 and split
    qkv_whole = jnp.transpose(qkv_weight, (1, 0, 2))
    qkv_half = lax.dynamic_slice_in_dim(qkv_whole, x * att, att, 2)
    out_half = lax.dynamic_slice_in_dim(out_weight, x * att, att, 0)
    if split:
        weights = [qkv_whole, out_weight, up_weight, down_weight]
        first_biases = [qkv_bias.reshape(3, 1, nx * att), up_bias.reshape(1, nx * ff)]
    else:
        up_half = lax.dynamic_slice_in_dim(up_weight, x * ff, ff, 1)
        down_half = lax.dynamic_slice_in_dim(down_weight, x * ff, ff, 0)
        weights = [qkv_half, out_half, up_half, down_half]
        first_biases = [
            lax.dynamic_slice_in_dim(qkv_bias, x * att, att, 1).reshape(3, 1, att),
            lax.dynamic_slice_in_dim(up_bias, x * ff, ff, 0).reshape(1, ff),
        ]

    frequency = np.exp(np.arange(ROT // 2) * (-2.0 / ROT) * ROPE_LOG_BASE).astype(np.float32)[:, None]

    if gather:
        sources = [block_input.reshape(rows * tokens, width), grad_output.reshape(rows * tokens, width)]
    else:
        sources = [lax.all_gather(a, "tensor", axis=2, tiled=True) for a in (block_input, grad_output)]
        sources = [lax.all_gather(a, "dp", axis=0, tiled=True).reshape(many, features) for a in sources]
    normed, cotangent, land, stats, down_part, d_hidden, branch_ff, up_bias_part, cos_t, sin_t, start, branch_y = front(
        gather, split, rows, tokens, nz, many, features, att, ff,
        [
            segment_ids, jnp.asarray(frequency), *sources, layer_norm_gain.reshape(1, features), layer_norm_bias.reshape(1, features), weights[0],
            first_biases[0], weights[1], weights[2], first_biases[1], weights[3],
        ],
    )
    home, sums, d_normed_ff, results = back(
        gather, split, tokens, land, cos_t, sin_t, start, cotangent, normed, weights[0], weights[1], branch_ff, branch_y,
        d_hidden, weights[2], down_part, block_input.reshape(rows * tokens, width),
        grad_output.reshape(rows * tokens, width), stats, layer_norm_gain.reshape(1, features), out_bias.reshape(1, width),
        down_bias.reshape(1, width), up_bias_part,
    )
    down_sum, up_sum, out_sum, qkv_sum = sums
    chunks = Chain.layout(weight_arrays(down_part.shape, d_hidden.shape, features, att))[0][-Chain.APART :]
    first = chunks[0][1]
    last_rows = lax.dynamic_slice(qkv_sum, (x, first, 0), (1, 3 * features - first, att))
    last_rows = lax.ppermute(last_rows, "dp", [(0, 1), (1, 0)])
    qkv_sum = lax.dynamic_update_slice(qkv_sum, last_rows, (1 - x, first, 0))
    if gather:
        block_output, input_grad, small = results
        block_output = block_output.reshape(rows, tokens, width)
        input_grad = input_grad.reshape(rows, tokens, width)
        gain_grad, shift_grad, bias_grad = small[0], small[1], small[2]
        units = nx * ff // width
        up_bias_grad = small[3 : 3 + units].reshape(nx * ff)
        qkv_bias_grad = small[3 + units : 6 + units]
    else:
        home = home.reshape(4, many, att)
        qkv_bias_part = jnp.sum(home[:3].astype(F32), axis=1)
        branch = branch_ff.astype(F32) + dot32(home[3], out_half)
        d_normed = d_normed_ff.astype(F32)
        for i in range(3):
            d_normed = d_normed + dot32(home[i], qkv_half[i].T)
        branch = scatter_sum(branch.reshape(all_rows, tokens, features))
        d_normed = scatter_sum(d_normed.reshape(all_rows, tokens, features))
        block_output = (block_input.astype(F32) + (branch + out_bias + down_bias)).astype(BF)

        stats = lax.dynamic_slice_in_dim(stats, x * rows * tokens, rows * tokens, 0).reshape(rows, tokens, 128)
        own_mean, own_inverse = stats[..., :1], stats[..., 64:65]
        xhat = (block_input.astype(F32) - own_mean) * own_inverse
        gain = lax.dynamic_slice_in_dim(layer_norm_gain, t * width, width, 0)
        scaled = d_normed * gain
        moments = jnp.stack([jnp.sum(scaled, axis=-1), jnp.sum(scaled * xhat, axis=-1)])
        moments = butterfly(moments, [("tensor", nt)]) / features
        first, second = moments[0][..., None], moments[1][..., None]
        input_grad = (
            grad_output.astype(F32) + own_inverse * (scaled - first - xhat * second)
        ).astype(BF)

        def spread(part, whole):
            shape = part.shape[:-1] + (whole,)
            at = (0,) * (part.ndim - 1) + (x * part.shape[-1],)
            return lax.dynamic_update_slice(jnp.zeros(shape, F32), part, at)

        small = [
            jnp.sum(d_normed * xhat, axis=(0, 1)),
            jnp.sum(d_normed, axis=(0, 1)),
            jnp.sum(grad_output.astype(F32), axis=(0, 1)),
            spread(up_bias_part[0], nx * ff),
            spread(qkv_bias_part, nx * att).reshape(-1),
        ]
        packed = butterfly(jnp.concatenate(small), [("dp", nx), ("blk", nz)])
        gain_grad, shift_grad, bias_grad = (packed[i * width : (i + 1) * width] for i in range(3))
        up_bias_grad = packed[3 * width : 3 * width + nx * ff]
        qkv_bias_grad = packed[3 * width + nx * ff :].reshape(3, nx * att)

    down_grad = widen_rows(down_sum)
    up_grad = widen_columns(up_sum)
    out_grad = widen_blocks(out_sum)
    qkv_grad = widen_columns(qkv_sum).reshape(3, features, nx * att)
    qkv_grad = jnp.transpose(qkv_grad, (1, 0, 2))
    return (
        block_output, input_grad, gain_grad, shift_grad, qkv_grad, qkv_bias_grad, out_grad, bias_grad, up_grad,
        up_bias_grad, down_grad, bias_grad,
    )


def solution(mesh):
    in_specs = (
        P("dp", "blk", "tensor"), P("dp", None), P(), P(), P(None, None, "tensor"), P(None, "tensor"), P("tensor", None),
        P("tensor"), P(None, "tensor"), P("tensor"), P("tensor", None), P("tensor"), P("dp", "blk", "tensor"),
    )
    out_specs = (
        P("dp", "blk", "tensor"), P("dp", "blk", "tensor"), P("tensor"), P("tensor"), P(None, None, "tensor"),
        P(None, "tensor"), P("tensor", None), P("tensor"), P(None, "tensor"), P("tensor"), P("tensor", None), P("tensor"),
    )
    body = functools.partial(local, mesh.shape["dp"], mesh.shape["blk"], mesh.shape["tensor"])
    return jax.shard_map(body, mesh=mesh, in_specs=in_specs, out_specs=out_specs, check_vma=False)
```

profile of v0, /device:TPU:0, one launch (start us, length us, event | category | flops | bytes accessed | tf_op | source)
XLA Modules:
  0.0 597.2 jit_solution(13218357580514725836)
XLA Ops:
  0.6 1.3 reshape.67.bq_ref
  1.9 122.4 %front.1 = (bf16[2048,2048]{1,0:T(8,128)(2,1)}, bf16[2048,2048]{1,0:T(8,128)(2,1)}, bf16[4,2048,256]{2,1,0:T(8,128)(2,1)}, f32[2048,128]{1,0:T(8,128)}, bf16[102...) custom-call(s32[2,2048]{1,0:T(2,128)} %segments_ref.1, ...), custom_call_target="tpu_custom_call" | custom-call | flops 60129542144 | bytes 104857600 | tf_op jit(solution)/shard_map/front/pallas_call | solution.py:460
  124.4 432.8 %back.1 = (bf16[4,4,512,256]{3,2,1,0:T(8,128)(2,1)}, bf16[2,1024,2048]{2,1,0:T(8,128)(2,1)}, bf16[2,2048,1024]{2,1,0:T(8,128)(2,1)}, bf16[2,1024,512]{2,1,0:T(8,...) custom-call(bf16[4,2048,256]{2,1,0:T(8,128)(2,1)} %get-tuple-element, ...), custom_call_target="tpu_custom_call" | custom-call | flops 51539607552 | bytes 536870912 | tf_op jit(solution)/shard_map/back/pallas_call | solution.py:1376
  557.1 1.2 constant_dynamic-slice_fusion
  558.3 0.1 collective-permute-start
  558.4 0.0 copy-start.1
  558.4 3.4 copy-done.1
  561.8 0.0 copy-start
  561.8 8.6 %widen.6 = f32[2048,2048]{1,0:T(8,128)} custom-call(bf16[2,2048,1024]{2,1,0:T(8,128)(2,1)S(1)} %copy-done.1), custom_call_target="tpu_custom_call" | custom-call | bytes 25165824 | tf_op jit(solution)/shard_map/widen/pallas_call | solution.py:1411
  570.4 0.0 copy-done
  570.4 0.0 copy-start.3
  570.5 8.6 %widen.7 = f32[2048,2048]{1,0:T(8,128)} custom-call(bf16[2,1024,2048]{2,1,0:T(8,128)(2,1)S(1)} %copy-done), custom_call_target="tpu_custom_call" | custom-call | bytes 25165824 | tf_op jit(solution)/shard_map/widen/pallas_call | solution.py:1411
  579.1 0.0 copy-start.6
  579.1 0.0 copy-done.3
  579.1 3.5 widen.5
  582.6 0.0 copy-done.6
  582.6 0.6 slice.17
  583.2 0.6 copy.26
  583.8 0.6 fusion
  584.4 0.0 copy-start.7
  584.4 0.0 collective-permute-done
  584.4 0.9 constant_dynamic-update-slice_fusion.source_ref
  585.3 0.0 copy-start.2
  585.3 2.8 copy-done.2
  588.1 0.0 copy-start.5
  588.1 0.0 copy-start.4
  588.1 6.6 %widen.4 = f32[6144,512]{1,0:T(8,128)} custom-call(bf16[2,6144,256]{2,1,0:T(8,128)(2,1)S(1)} %copy-done.2), custom_call_target="tpu_custom_call" | custom-call | bytes 18874368 | tf_op jit(solution)/shard_map/widen/pallas_call | solution.py:1411
  594.7 0.0 copy-done.7
  594.7 0.6 copy.31
  595.2 0.0 copy-done.5
  595.2 1.0 copy.32
  596.2 0.0 copy-done.4
  596.2 1.0 copy.33
  (1 shorter events, 0.0 us)
Async XLA Ops:
  558.3 26.0 %collective-permute-start = (bf16[1,1536,256]{2,1,0:T(8,128)(2,1)S(1)}, bf16[1,1536,256]{2,1,0:T(8,128)(2,1)S(1)}, u32[]{:S(2)}, u32[]{:S(2)}) collective-permute-start(bf16[1,1536,256]{2,1,0:T(8,128)(2,1)S(1)} %constant_dynamic-slice_fusion), channel_id=1, source_target_pairs={{0,16},{16,0},{1,17},{17,1},{2,18},{18,2},{3,19},{19,3},{4,20},{20... | collective-permute-start | bytes 2359304 | tf_op jit(solution)/shard_map/ppermute | solution.py:1522
  558.4 3.4 copy-start.1
  561.8 8.6 %copy-start = (bf16[2,1024,2048]{2,1,0:T(8,128)(2,1)S(1)}, bf16[2,1024,2048]{2,1,0:T(8,128)(2,1)}, u32[]{:S(2)}) copy-start(bf16[2,1024,2048]{2,1,0:T(8,128)(2,1)} %get-tuple-element.49.source_ref) | copy-start | bytes 25165828
  570.4 8.6 %copy-start.3 = (bf16[2,1024,512]{2,1,0:T(8,128)(2,1)S(1)}, bf16[2,1024,512]{2,1,0:T(8,128)(2,1)}, u32[]{:S(2)}) copy-start(bf16[2,1024,512]{2,1,0:T(8,128)(2,1)} %get-tuple-element.47.source_ref) | copy-start | bytes 6291460
  579.1 3.5 copy-start.6
  584.4 10.3 %copy-start.7 = (f32[1,512]{1,0:T(1,128)}, f32[1,512]{1,0:T(1,128)S(1)}, u32[]{:S(2)}) copy-start(f32[1,512]{1,0:T(1,128)S(1)} %get-tuple-element.50) | copy-start | bytes 6148
  585.3 2.8 copy-start.2
  588.1 7.2 %copy-start.5 = (bf16[1024,512]{1,0:T(8,128)(2,1)S(1)}, bf16[1024,512]{1,0:T(8,128)(2,1)}, u32[]{:S(2)}) copy-start(bf16[1024,512]{1,0:T(8,128)(2,1)} %get-tuple-element.43) | copy-start | bytes 3145732
  588.1 8.1 %copy-start.4 = (bf16[1024,512]{1,0:T(8,128)(2,1)S(1)}, bf16[1024,512]{1,0:T(8,128)(2,1)}, u32[]{:S(2)}) copy-start(bf16[1024,512]{1,0:T(8,128)(2,1)} %get-tuple-element.44) | copy-start | bytes 3145732
where the time goes:
time: 599 us; the launch traced here: 597 us
  Pallas kernels  583 us (97%)
  local copies, waits for them, and re-layouts  13.9 us (2%)
    pallas_call x1, Pallas kernels, back(): pl.pallas_call(functools.partial(back_kernel, arrays, scatter, split, hea...  433 us
    pallas_call x1, Pallas kernels, front(): pl.pallas_call(functools.partial(front_kernel, gather, split, rows, token...  122 us
    pallas_call x4, Pallas kernels, widen(): pl.pallas_call(body, out_shape=jax.ShapeDtypeStruct(out_shape, F32), grid...  27.3 us
  transfers between devices with their start and end apart: 1, of which 0 were waited for; matrix products, arithmetic and copies ran while one was open for 0% of the time, Pallas kernels for 3%

commit v1 on v0

--- a/solution.py
+++ b/solution.py
@@ -520,7 +520,7 @@
     END_LAG = 5
     MID_LAG = 2
     INWARD = 2
-    APART = 3
+    APART = 5
     ASIDE = 8
 
     @classmethod

time: 599 us -> 590 us (0.985)
  Pallas kernels: 583 us -> 571 us
    pallas_call x1, Pallas kernels: 433 us -> 422 us  [back(): pl.pallas_call(functools.partial(back_kernel, arrays, scatter, split, hea...]
  transfers between devices with their start and end apart: 1 -> 1, of which waited for: 0 -> 1; matrix products, arithmetic and copies ran while one was open for 0% -> 0% of each run, Pallas kernels for 3% -> 4%
where the time goes in v1:
time: 590 us; the launch traced here: 588 us
  Pallas kernels  571 us (97%)
  local copies, waits for them, and re-layouts  14.3 us (2%)
    pallas_call x1, Pallas kernels, back(): pl.pallas_call(functools.partial(back_kernel, arrays, scatter, split, hea...  422 us
    pallas_call x1, Pallas kernels, front(): pl.pallas_call(functools.partial(front_kernel, gather, split, rows, token...  122 us
    pallas_call x4, Pallas kernels, widen(): pl.pallas_call(body, out_shape=jax.ShapeDtypeStruct(out_shape, F32), grid...  27.3 us
  transfers between devices with their start and end apart: 1, of which 1 were waited for; matrix products, arithmetic and copies ran while one was open for 0% of the time, Pallas kernels for 4%

profile of v1, /device:TPU:0, one launch (start us, length us, event | category | flops | bytes accessed | tf_op | source)
XLA Modules:
  0.0 587.5 jit_solution(1507704386235825439)
XLA Ops:
  0.6 1.3 reshape.67.bq_ref
  1.9 122.4 %front.1 = (bf16[2048,2048]{1,0:T(8,128)(2,1)}, bf16[2048,2048]{1,0:T(8,128)(2,1)}, bf16[4,2048,256]{2,1,0:T(8,128)(2,1)}, f32[2048,128]{1,0:T(8,128)}, bf16[102...) custom-call(s32[2,2048]{1,0:T(2,128)} %segments_ref.1, ...), custom_call_target="tpu_custom_call" | custom-call | flops 60129542144 | bytes 104857600 | tf_op jit(solution)/shard_map/front/pallas_call | solution.py:460
  124.4 421.5 %back.1 = (bf16[4,4,512,256]{3,2,1,0:T(8,128)(2,1)}, bf16[2,1024,2048]{2,1,0:T(8,128)(2,1)}, bf16[2,2048,1024]{2,1,0:T(8,128)(2,1)}, bf16[2,1024,512]{2,1,0:T(8,...) custom-call(bf16[4,2048,256]{2,1,0:T(8,128)(2,1)} %get-tuple-element, ...), custom_call_target="tpu_custom_call" | custom-call | flops 51539607552 | bytes 536870912 | tf_op jit(solution)/shard_map/back/pallas_call | solution.py:1376
  545.9 1.4 constant_dynamic-slice_fusion
  547.3 0.1 collective-permute-start
  547.4 0.0 copy-start.2
  547.4 3.4 copy-done.2
  550.8 0.0 copy-start.1
  550.8 8.6 %widen.6 = f32[2048,2048]{1,0:T(8,128)} custom-call(bf16[2,2048,1024]{2,1,0:T(8,128)(2,1)S(1)} %copy-done.2), custom_call_target="tpu_custom_call" | custom-call | bytes 25165824 | tf_op jit(solution)/shard_map/widen/pallas_call | solution.py:1411
  559.4 0.0 copy-done.1
  559.4 0.0 copy-start.3
  559.4 8.6 %widen.7 = f32[2048,2048]{1,0:T(8,128)} custom-call(bf16[2,1024,2048]{2,1,0:T(8,128)(2,1)S(1)} %copy-done.1), custom_call_target="tpu_custom_call" | custom-call | bytes 25165824 | tf_op jit(solution)/shard_map/widen/pallas_call | solution.py:1411
  568.1 0.0 copy-start.6
  568.1 0.0 copy-done.3
  568.1 3.5 widen.5
  571.6 0.0 copy-done.6
  571.6 0.6 slice.17
  572.2 0.6 copy.26
  572.8 0.6 fusion
  573.4 0.0 copy-start.7
  573.4 1.2 collective-permute-done
  574.5 1.1 constant_dynamic-update-slice_fusion.source_ref
  575.6 0.0 copy-start
  575.6 2.8 copy-done
  578.4 0.0 copy-start.5
  578.4 0.0 copy-start.4
  578.4 6.6 %widen.4 = f32[6144,512]{1,0:T(8,128)} custom-call(bf16[2,6144,256]{2,1,0:T(8,128)(2,1)S(1)} %copy-done), custom_call_target="tpu_custom_call" | custom-call | bytes 18874368 | tf_op jit(solution)/shard_map/widen/pallas_call | solution.py:1411
  585.0 0.0 copy-done.7
  585.0 0.6 copy.31
  585.6 0.0 copy-done.5
  585.6 1.0 copy.32
  586.6 0.0 copy-done.4
  586.6 1.0 copy.33
  (1 shorter events, 0.0 us)
Async XLA Ops:
  547.3 27.2 %collective-permute-start = (bf16[1,2560,256]{2,1,0:T(8,128)(2,1)S(1)}, bf16[1,2560,256]{2,1,0:T(8,128)(2,1)S(1)}, u32[]{:S(2)}, u32[]{:S(2)}) collective-permute-start(bf16[1,2560,256]{2,1,0:T(8,128)(2,1)S(1)} %constant_dynamic-slice_fusion), channel_id=1, source_target_pairs={{0,16},{16,0},{1,17},{17,1},{2,18},{18,2},{3,19},{19,3},{4,20},{20... | collective-permute-start | bytes 3932168 | tf_op jit(solution)/shard_map/ppermute | solution.py:1522
  547.4 3.4 copy-start.2
  550.8 8.6 %copy-start.1 = (bf16[2,1024,2048]{2,1,0:T(8,128)(2,1)S(1)}, bf16[2,1024,2048]{2,1,0:T(8,128)(2,1)}, u32[]{:S(2)}) copy-start(bf16[2,1024,2048]{2,1,0:T(8,128)(2,1)} %get-tuple-element.49.source_ref) | copy-start | bytes 25165828
  559.4 8.6 %copy-start.3 = (bf16[2,1024,512]{2,1,0:T(8,128)(2,1)S(1)}, bf16[2,1024,512]{2,1,0:T(8,128)(2,1)}, u32[]{:S(2)}) copy-start(bf16[2,1024,512]{2,1,0:T(8,128)(2,1)} %get-tuple-element.47.source_ref) | copy-start | bytes 6291460
  568.1 3.5 copy-start.6
  573.4 11.6 %copy-start.7 = (f32[1,512]{1,0:T(1,128)}, f32[1,512]{1,0:T(1,128)S(1)}, u32[]{:S(2)}) copy-start(f32[1,512]{1,0:T(1,128)S(1)} %get-tuple-element.50) | copy-start | bytes 6148
  575.6 2.8 copy-start
  578.4 7.2 %copy-start.5 = (bf16[1024,512]{1,0:T(8,128)(2,1)S(1)}, bf16[1024,512]{1,0:T(8,128)(2,1)}, u32[]{:S(2)}) copy-start(bf16[1024,512]{1,0:T(8,128)(2,1)} %get-tuple-element.43) | copy-start | bytes 3145732
  578.4 8.1 %copy-start.4 = (bf16[1024,512]{1,0:T(8,128)(2,1)S(1)}, bf16[1024,512]{1,0:T(8,128)(2,1)}, u32[]{:S(2)}) copy-start(bf16[1024,512]{1,0:T(8,128)(2,1)} %get-tuple-element.44) | copy-start | bytes 3145732

commit v2 on v1

--- a/solution.py
+++ b/solution.py
@@ -305,7 +305,8 @@
     def project(row):
         @pl.loop(0, 3)
         def _(part):
-            bias = bq_ref[part, :, pl.ds(pl.multiple_of(x * att, 128), att)] if split else bq_ref[part]
+            lanes = pl.ds(pl.multiple_of(x * att, 128), att) if split else slice(None)
+            bias = bq_ref[pl.ds(part, 1), lanes]
             value = dot32(xin[place(row), :], vq[part]) + bias
             pay[row, part] = value.astype(BF)
 
@@ -1485,13 +1486,13 @@
     out_half = lax.dynamic_slice_in_dim(out_weight, x * att, att, 0)
     if split:
         weights = [qkv_whole, out_weight, up_weight, down_weight]
-        first_biases = [qkv_bias.reshape(3, 1, nx * att), up_bias.reshape(1, nx * ff)]
+        first_biases = [qkv_bias, up_bias.reshape(1, nx * ff)]
     else:
         up_half = lax.dynamic_slice_in_dim(up_weight, x * ff, ff, 1)
         down_half = lax.dynamic_slice_in_dim(down_weight, x * ff, ff, 0)
         weights = [qkv_half, out_half, up_half, down_half]
         first_biases = [
-            lax.dynamic_slice_in_dim(qkv_bias, x * att, att, 1).reshape(3, 1, att),
+            lax.dynamic_slice_in_dim(qkv_bias, x * att, att, 1),
             lax.dynamic_slice_in_dim(up_bias, x * ff, ff, 0).reshape(1, ff),
         ]
 

time: 590 us -> 588 us (level)
  no operation moved by 1% of the time
where the time goes in v2:
time: 588 us; the launch traced here: 586 us
  Pallas kernels  571 us (97%)
  local copies, waits for them, and re-layouts  13 us (2%)
    pallas_call x1, Pallas kernels, back(): pl.pallas_call(functools.partial(back_kernel, arrays, scatter, split, hea...  422 us
    pallas_call x1, Pallas kernels, front(): pl.pallas_call(functools.partial(front_kernel, gather, split, rows, token...  122 us
    pallas_call x4, Pallas kernels, widen(): pl.pallas_call(body, out_shape=jax.ShapeDtypeStruct(out_shape, F32), grid...  27.3 us
  transfers between devices with their start and end apart: 1, of which 1 were waited for; matrix products, arithmetic and copies ran while one was open for 0% of the time, Pallas kernels for 4%

profile of v2, /device:TPU:0, one launch (start us, length us, event | category | flops | bytes accessed | tf_op | source)
XLA Modules:
  0.0 586.3 jit_solution(18003251331481046126)
XLA Ops:
  0.6 122.5 %front.1 = (bf16[2048,2048]{1,0:T(8,128)(2,1)}, bf16[2048,2048]{1,0:T(8,128)(2,1)}, bf16[4,2048,256]{2,1,0:T(8,128)(2,1)}, f32[2048,128]{1,0:T(8,128)}, bf16[102...) custom-call(s32[2,2048]{1,0:T(2,128)} %segments_ref.1, ...), custom_call_target="tpu_custom_call" | custom-call | flops 60129542144 | bytes 104857600 | tf_op jit(solution)/shard_map/front/pallas_call | solution.py:461
  123.1 421.5 %back.1 = (bf16[4,4,512,256]{3,2,1,0:T(8,128)(2,1)}, bf16[2,1024,2048]{2,1,0:T(8,128)(2,1)}, bf16[2,2048,1024]{2,1,0:T(8,128)(2,1)}, bf16[2,1024,512]{2,1,0:T(8,...) custom-call(bf16[4,2048,256]{2,1,0:T(8,128)(2,1)} %get-tuple-element, ...), custom_call_target="tpu_custom_call" | custom-call | flops 51539607552 | bytes 536870912 | tf_op jit(solution)/shard_map/back/pallas_call | solution.py:1377
  544.6 1.4 constant_dynamic-slice_fusion
  546.1 0.1 collective-permute-start
  546.1 0.0 copy-start.2
  546.2 3.4 copy-done.2
  549.5 0.0 copy-start.1
  549.5 8.6 %widen.6 = f32[2048,2048]{1,0:T(8,128)} custom-call(bf16[2,2048,1024]{2,1,0:T(8,128)(2,1)S(1)} %copy-done.2), custom_call_target="tpu_custom_call" | custom-call | bytes 25165824 | tf_op jit(solution)/shard_map/widen/pallas_call | solution.py:1412
  558.2 0.0 copy-done.1
  558.2 0.0 copy-start.3
  558.2 8.6 %widen.7 = f32[2048,2048]{1,0:T(8,128)} custom-call(bf16[2,1024,2048]{2,1,0:T(8,128)(2,1)S(1)} %copy-done.1), custom_call_target="tpu_custom_call" | custom-call | bytes 25165824 | tf_op jit(solution)/shard_map/widen/pallas_call | solution.py:1412
  566.8 0.0 copy-start.6
  566.8 0.0 copy-done.3
  566.8 3.5 widen.5
  570.3 0.0 copy-done.6
  570.3 0.6 slice.17
  570.9 0.6 copy.26
  571.5 0.6 fusion
  572.1 0.0 copy-start.7
  572.1 1.2 collective-permute-done
  573.3 1.1 constant_dynamic-update-slice_fusion.source_ref
  574.4 0.0 copy-start
  574.4 2.8 copy-done
  577.2 0.0 copy-start.5
  577.2 0.0 copy-start.4
  577.2 6.6 %widen.4 = f32[6144,512]{1,0:T(8,128)} custom-call(bf16[2,6144,256]{2,1,0:T(8,128)(2,1)S(1)} %copy-done), custom_call_target="tpu_custom_call" | custom-call | bytes 18874368 | tf_op jit(solution)/shard_map/widen/pallas_call | solution.py:1412
  583.7 0.0 copy-done.7
  583.7 0.6 copy.31
  584.3 0.0 copy-done.5
  584.3 1.0 copy.32
  585.3 0.0 copy-done.4
  585.3 1.0 copy.33
  (1 shorter events, 0.0 us)
Async XLA Ops:
  546.1 27.2 %collective-permute-start = (bf16[1,2560,256]{2,1,0:T(8,128)(2,1)S(1)}, bf16[1,2560,256]{2,1,0:T(8,128)(2,1)S(1)}, u32[]{:S(2)}, u32[]{:S(2)}) collective-permute-start(bf16[1,2560,256]{2,1,0:T(8,128)(2,1)S(1)} %constant_dynamic-slice_fusion), channel_id=1, source_target_pairs={{0,16},{16,0},{1,17},{17,1},{2,18},{18,2},{3,19},{19,3},{4,20},{20... | collective-permute-start | bytes 3932168 | tf_op jit(solution)/shard_map/ppermute | solution.py:1523
  546.1 3.4 copy-start.2
  549.5 8.6 %copy-start.1 = (bf16[2,1024,2048]{2,1,0:T(8,128)(2,1)S(1)}, bf16[2,1024,2048]{2,1,0:T(8,128)(2,1)}, u32[]{:S(2)}) copy-start(bf16[2,1024,2048]{2,1,0:T(8,128)(2,1)} %get-tuple-element.49.source_ref) | copy-start | bytes 25165828
  558.2 8.6 %copy-start.3 = (bf16[2,1024,512]{2,1,0:T(8,128)(2,1)S(1)}, bf16[2,1024,512]{2,1,0:T(8,128)(2,1)}, u32[]{:S(2)}) copy-start(bf16[2,1024,512]{2,1,0:T(8,128)(2,1)} %get-tuple-element.47.source_ref) | copy-start | bytes 6291460
  566.8 3.5 copy-start.6
  572.1 11.6 %copy-start.7 = (f32[1,512]{1,0:T(1,128)}, f32[1,512]{1,0:T(1,128)S(1)}, u32[]{:S(2)}) copy-start(f32[1,512]{1,0:T(1,128)S(1)} %get-tuple-element.50) | copy-start | bytes 6148
  574.4 2.8 copy-start
  577.2 7.2 %copy-start.5 = (bf16[1024,512]{1,0:T(8,128)(2,1)S(1)}, bf16[1024,512]{1,0:T(8,128)(2,1)}, u32[]{:S(2)}) copy-start(bf16[1024,512]{1,0:T(8,128)(2,1)} %get-tuple-element.43) | copy-start | bytes 3145732
  577.2 8.1 %copy-start.4 = (bf16[1024,512]{1,0:T(8,128)(2,1)S(1)}, bf16[1024,512]{1,0:T(8,128)(2,1)}, u32[]{:S(2)}) copy-start(bf16[1024,512]{1,0:T(8,128)(2,1)} %get-tuple-element.44) | copy-start | bytes 3145732
